TPU v7x, 32 devices: a whole 2x2x4 slice. The times are simulated.
32 devices in a mesh: patch: 8 (over z, x), tile: 4 (over y, core).
Axes of the slice: x: 2, y: 2, z: 4, core: 2. Of those that a mesh axis runs over, the one named last changes fastest.
Arguments:
- latents: float32 [1088, 128], P('patch')
- timestamps: int32 [1088], P('patch'), may hold values from 0 to 56, as said below
- cell_map: int32 [1024], replicated, may hold values from 0 to 1023, as said below
- w_video: bfloat16 [128, 3072], replicated, may hold values from -0.5 to 0.5
- w_audio: bfloat16 [128, 3072], replicated, may hold values from -0.5 to 0.5
- mod_scale: float32 [2, 3072], replicated, may hold values from -3 to 3
- mod_shift: float32 [2, 3072], replicated, may hold values from -3 to 3
- w_query: bfloat16 [3072, 3072], P(None, 'tile')
- w_key: bfloat16 [3072, 3072], P(None, 'tile')
- w_value: bfloat16 [3072, 3072], P(None, 'tile'), may hold values from -0.109375 to 0.109375
- q_gain: float32 [3072], P('tile'), as said below
- k_gain: float32 [3072], P('tile'), as said below
- k_cache: bfloat16 [1088, 3072], P('patch', 'tile'), may hold values from -8 to 8
- v_cache: bfloat16 [1088, 3072], P('patch', 'tile'), may hold values from -6 to 6
- w_out: bfloat16 [3072, 3072], P('tile'), may hold values from -0.109375 to 0.109375
- out_gain: float32 [3072], replicated, may hold values from 0.25 to 1.75
- w_final: bfloat16 [3072, 128], replicated, may hold values from -0.109375 to 0.109375
- step_sizes: float32 [2], replicated, may hold values from 0.2 to 0.6
- conv_w: bfloat16 [3, 3, 3, 128, 512], replicated, may hold values from -0.109375 to 0.109375
- conv_b: float32 [512], replicated, may hold values from -3 to 3
Outputs:
- final_latents: float32 [1088, 128], P('patch')
- decoded: bfloat16 [8, 16, 8, 512], P(None, 'patch', 'tile')
Inputs may be any that keep to these rules, and one draw needn't show every extreme that they name: `cell_map`: a permutation of the 1024 cells of the grid; entry r is the cell of the r-th video token, which stands in patch shard r // 128; cell (f, h, w) belongs to the decode block (h // 2, w // 2), held by patch index h // 2 and tile index w // 2; every patch shard holds exactly 4 cells of every decode block. A video token's timestamp is 8 times the frame of its cell; audio tokens' timestamps lie in the same span. `q_gain`: positive. `k_gain`: positive.
All inputs are finite; a program needn't handle non-finite values.
Results may differ from a plain program's by a relative error of at most 0.009.
Values may be sent and summed in bfloat16 or wider, within the bound.
A program may use at most 128 MiB of HBM per device.

v0:
```python
import jax
import jax.numpy as jnp
from jax import lax
from jax.sharding import PartitionSpec as P

HEAD = 128
VID_DEV = 128
STEPS = 2
FRAMES = 8
BH = 2
EPSILON = 1e-06


def with_halo(shard, sides, width):
    for axis, dim in sides:
        count, length = (lax.axis_size(axis), shard.shape[dim])
        up = [(i, (i + 1) % count) for i in range(count - 1)]
        down = [(j, i) for i, j in up]
        last = lax.slice_in_dim(shard, length - width, length, axis=dim)
        first = lax.slice_in_dim(shard, 0, width, axis=dim)
        before = lax.ppermute(last, axis, up)
        after = lax.ppermute(first, axis, down)
        shard = jnp.concatenate([before, shard, after], axis=dim)
    return shard


def row_scaled(matrix):
    return matrix * lax.rsqrt(jnp.mean(matrix * matrix, axis=-1, keepdims=True) + EPSILON)


def rotate(matrix, stamps):
    half_size = matrix.shape[-1] // 2
    frequency = jnp.exp(-jnp.log(10000.0) * jnp.arange(half_size, dtype=jnp.float32) / half_size)
    angles = stamps.astype(jnp.float32)[:, None, None] * frequency
    cosine = jnp.cos(angles)
    sines = jnp.sin(angles)
    leading = matrix[..., :half_size]
    trailing = matrix[..., half_size:]
    return jnp.concatenate(
        [leading * cosine - trailing * sines, leading * sines + trailing * cosine], axis=-1
    )


def head_project(normed, weight, gain, stamps):
    raw_out = jnp.dot(normed, weight, preferred_element_type=jnp.float32)
    shaped = raw_out.reshape(raw_out.shape[0], -1, HEAD)
    scaled = row_scaled(shaped) * gain.reshape(-1, HEAD)
    return rotate(scaled, stamps).reshape(raw_out.shape[0], -1).astype(jnp.bfloat16)


def attend_whole(queries, fresh_keys, values, stale_keys, stale_values, row_start):
    every_keys, every_values = (
        lax.all_gather(stale_keys, "patch", axis=0, tiled=True),
        lax.all_gather(stale_values, "patch", axis=0, tiled=True),
    )
    every_keys = lax.dynamic_update_slice_in_dim(every_keys, fresh_keys, row_start, 0)
    every_values = lax.dynamic_update_slice_in_dim(every_values, values, row_start, 0)
    row_count = queries.shape[0]
    query_heads = queries.reshape(row_count, -1, HEAD)
    key_heads = every_keys.reshape(every_keys.shape[0], -1, HEAD)
    value_heads = every_values.reshape(every_values.shape[0], -1, HEAD)
    scores = jnp.einsum(
        "qhd,khd->hqk", query_heads, key_heads, preferred_element_type=jnp.float32
    ) * HEAD ** (-0.5)
    row_top = jnp.max(scores, axis=2, keepdims=True)
    weights = jnp.exp(scores - row_top)
    totals = jnp.sum(weights, axis=2)
    result = jnp.einsum(
        "hqk,khd->qhd",
        weights.astype(jnp.bfloat16),
        value_heads,
        preferred_element_type=jnp.float32,
    )
    return (result / totals.T[:, :, None]).reshape(row_count, -1).astype(jnp.bfloat16)


def velocity_of(embedded, attended, w_out, out_gain, w_final):
    share_rows = attended.shape[0] // lax.axis_size("tile")
    own_rows = lax.dynamic_slice_in_dim(
        embedded, lax.axis_index("tile") * share_rows, share_rows, 0
    )
    mixed_rows = own_rows + lax.psum_scatter(
        jnp.dot(attended, w_out, preferred_element_type=jnp.float32).astype(jnp.bfloat16),
        "tile",
        scatter_dimension=0,
        tiled=True,
    ).astype(jnp.float32)
    final_normed = (row_scaled(mixed_rows) * out_gain).astype(jnp.bfloat16)
    own_velocity = jnp.dot(final_normed, w_final, preferred_element_type=jnp.float32)
    return lax.all_gather(own_velocity, "tile", axis=0, tiled=True)


def decode(latent_state, cell_map, conv_w, conv_b):
    video_rows = latent_state[:VID_DEV].astype(jnp.bfloat16)
    patch_count = lax.axis_size("patch")
    tile_count = lax.axis_size("tile")
    patch_index = lax.axis_index("patch")
    tile_index = lax.axis_index("tile")
    block_width = VID_DEV // (tile_count * FRAMES * BH)
    grid_rows = BH * patch_count
    grid_columns = block_width * tile_count
    cell_count = FRAMES * BH * block_width
    local_cells = jnp.arange(cell_count, dtype=jnp.int32)
    frame_ids = local_cells // (BH * block_width)
    inner_row = local_cells // block_width % BH
    inner_column = local_cells % block_width
    own_cells = (
        (frame_ids * grid_rows + patch_index * BH + inner_row) * grid_columns
        + tile_index * block_width
        + inner_column
    )
    matches = cell_map[None, :] == own_cells[:, None]
    every_video = lax.all_gather(video_rows, "patch", axis=0, tiled=True)
    sources = jnp.sum(
        jnp.where(matches, jnp.arange(cell_map.shape[0], dtype=jnp.int32)[None, :], 0), axis=1
    )
    block = every_video[sources]
    block = block.reshape(FRAMES, BH, block_width, -1)
    grown = with_halo(block, (("patch", 1), ("tile", 2)), 1)
    padded = jnp.pad(grown, ((1, 1), (0, 0), (0, 0), (0, 0)))
    columns = jnp.concatenate(
        [
            padded[
                shift_time : shift_time + FRAMES,
                shift_row : shift_row + BH,
                shift_column : shift_column + block_width,
            ]
            for shift_time in range(3)
            for shift_row in range(3)
            for shift_column in range(3)
        ],
        axis=-1,
    )
    kernel = conv_w.reshape(-1, conv_w.shape[-1])
    conv_out = (
        jnp.dot(columns.reshape(cell_count, -1), kernel, preferred_element_type=jnp.float32)
        + conv_b
    )
    return conv_out.astype(jnp.bfloat16).reshape(FRAMES, BH, block_width, -1)


def local(
    latents,
    timestamps,
    cell_map,
    w_video,
    w_audio,
    mod_scale,
    mod_shift,
    w_query,
    w_key,
    w_value,
    q_gain,
    k_gain,
    k_cache,
    v_cache,
    w_out,
    out_gain,
    w_final,
    step_sizes,
    conv_w,
    conv_b,
):
    row_count = latents.shape[0]
    row_start = lax.axis_index("patch") * row_count
    latent_state = latents
    stale_keys = k_cache
    stale_values = v_cache
    for step_index in range(STEPS):
        latent_b = latent_state.astype(jnp.bfloat16)
        video_part = jnp.dot(latent_b[:VID_DEV], w_video, preferred_element_type=jnp.float32)
        audio_part = jnp.dot(latent_b[VID_DEV:], w_audio, preferred_element_type=jnp.float32)
        embedded = jnp.concatenate([video_part, audio_part], axis=0)
        normed = (
            row_scaled(embedded) * (1.0 + mod_scale[step_index]) + mod_shift[step_index]
        ).astype(jnp.bfloat16)
        queries = head_project(normed, w_query, q_gain, timestamps)
        fresh_keys = head_project(normed, w_key, k_gain, timestamps)
        values = jnp.dot(normed, w_value, preferred_element_type=jnp.float32).astype(jnp.bfloat16)
        attended = attend_whole(queries, fresh_keys, values, stale_keys, stale_values, row_start)
        velocity = velocity_of(embedded, attended, w_out, out_gain, w_final)
        latent_state = latent_state - step_sizes[step_index] * velocity
        stale_keys = fresh_keys
        stale_values = values
    decoded = decode(latent_state, cell_map, conv_w, conv_b)
    return (latent_state, decoded)


def solution(mesh):
    return jax.shard_map(
        local,
        mesh=mesh,
        in_specs=(
            P("patch", None),
            P("patch"),
            P(),
            P(),
            P(),
            P(),
            P(),
            P(None, "tile"),
            P(None, "tile"),
            P(None, "tile"),
            P("tile"),
            P("tile"),
            P("patch", "tile"),
            P("patch", "tile"),
            P("tile", None),
            P(),
            P(),
            P(),
            P(),
            P(),
        ),
        out_specs=(P("patch", None), P(None, "patch", "tile", None)),
        check_vma=False,
    )
```

profile of v0, /device:TPU:12, one launch (start us, length us, event | category | flops | bytes accessed | tf_op | source)
XLA Modules:
  0.0 313.6 jit_solution(8176964901523891090)
XLA Ops:
  18.8 1.9 multiply_reduce_fusion.4
  21.7 4.2 %fusion.94 = f32[136,768]{1,0:T(8,128)} fusion(bf16[136,3072]{1,0:T(8,128)(2,1)} %copy-done.7, bf16[3072,768]{1,0:T(8,128)(2,1)} %param.27), kind=kOutput, calls=%fused_computation.194 | convolution fusion | flops 641728512 | bytes 5971968 | tf_op jit(solution)/shard_map/dot_general | solution.py:45
  38.1 18.7 %all-gather.7.cloned.1.call-done = bf16[1088,768]{1,0:T(8,128)(2,1)} async-done(((bf16[136,768]{1,0:T(8,128)(2,1)}), bf16[1088,768]{1,0:T(8,128)(2,1)}) %all-gather.7.cloned.1.call-update) | async-done | bytes 1671184 | tf_op jit(solution)/shard_map/all_gather | solution.py:54
  56.8 4.2 %constant_dynamic-update-slice_fusion.28 = (bf16[1088,768]{1,0:T(8,128)(2,1)}, bf16[136,768]{1,0:T(8,128)(2,1)}) fusion(bf16[1088,768]{1,0:T(8,128)(2,1)} %all-gather.7.cloned.1.call-done, s32[]{:T(128)S(6)} %select_n.60, bf16[136,3072]{1,0:T(8,128)(2,1)} %copy-done.7, bf16[3072,768]{1,0:T(8,128)(2,1)} %param.29), kind=kOutput, calls=%fused_computation.161 | convolution fusion | flops 641832960 | bytes 5971972 | tf_op jit(solution)/shard_map/dot_general | solution.py:179
  61.0 3.8 %copy.84 = bf16[1088,768]{0,1:T(8,128)(2,1)} copy(bf16[1088,768]{1,0:T(8,128)(2,1)} %get-tuple-element.54) | data formatting | bytes 3342336 | tf_op jit(solution)/shard_map/dynamic_update_slice | solution.py:57
  64.9 38.1 %all-gather.9.cloned.1.call-done = bf16[1088,768]{1,0:T(8,128)(2,1)} async-done(((bf16[136,768]{1,0:T(8,128)(2,1)}), bf16[1088,768]{1,0:T(8,128)(2,1)}) %all-gather.9.cloned.1.call-update) | async-done | bytes 1671184 | tf_op jit(solution)/shard_map/all_gather | solution.py:53
  104.8 3.8 %copy.90 = bf16[1088,768]{0,1:T(8,128)(2,1)} copy(bf16[1088,768]{1,0:T(8,128)(2,1)} %constant_dynamic-update-slice_fusion.27) | data formatting | bytes 3342336 | tf_op jit(solution)/shard_map/dynamic_update_slice | solution.py:56
  108.6 2.7 fusion.92
  115.7 14.3 %fusion = bf16[40,3072]{1,0:T(8,128)(2,1)} fusion(bf16[136,3072]{1,0:T(8,128)(2,1)} %convolution_convert_fusion.1), kind=kCustom, calls=%all-reduce-scatter | all-reduce-scatter fusion | flops 491521 | bytes 1081856
  134.2 4.2 %collective-permute-done.4 = bf16[18,3072]{1,0:T(8,128)(2,1)} collective-permute-done((bf16[18,3072]{1,0:T(8,128)(2,1)}, bf16[18,3072]{1,0:T(8,128)(2,1)}, u32[]{:S(2)}, u32[]{:S(2)}) %collective-permute-start.4) | collective-permute-done | bytes 110624
  138.4 5.4 %concatenate.139 = bf16[58,3072]{1,0:T(8,128)(2,1)} concatenate(bf16[18,3072]{1,0:T(8,128)(2,1)} %collective-permute-done.4, bf16[40,3072]{1,0:T(8,128)(2,1)} %fusion), dimensions={0} | concatenate | bytes 712704
  147.2 5.5 %all-gather = f32[4,34,128]{2,1,0:T(8,128)S(1)} all-gather(f32[1,34,128]{2,1,0:T(8,128)S(1)} %convolution_bitcast_fusion.1), channel_id=1, replica_groups=mesh['patch'=8,'tile'=4] {'tile'}, dimensions={0}, use_global_device_ids=true | all-gather | bytes 87040 | tf_op jit(solution)/shard_map/all_gather | solution.py:90
  162.1 4.0 %fusion.96 = f32[136,768]{1,0:T(8,128)} fusion(bf16[136,3072]{1,0:T(8,128)(2,1)S(1)} %add_convert_fusion, bf16[3072,768]{1,0:T(8,128)(2,1)} %param.27), kind=kOutput, calls=%fused_computation.196 | convolution fusion | flops 641728512 | bytes 5971968 | tf_op jit(solution)/shard_map/dot_general | solution.py:45
  171.4 4.2 %fusion.97 = f32[136,768]{1,0:T(8,128)} fusion(bf16[136,3072]{1,0:T(8,128)(2,1)} %copy-done.8, bf16[3072,768]{1,0:T(8,128)(2,1)} %param.28), kind=kOutput, calls=%fused_computation.197 | convolution fusion | flops 641728512 | bytes 5971968 | tf_op jit(solution)/shard_map/dot_general | solution.py:45
  175.6 1.9 reshape.274
  188.0 3.8 %copy.100 = bf16[1088,768]{0,1:T(8,128)(2,1)} copy(bf16[1088,768]{1,0:T(8,128)(2,1)} %bitcast_dynamic-update-slice_fusion) | data formatting | bytes 3342336 | tf_op jit(solution)/shard_map/dynamic_update_slice | solution.py:56
  191.8 2.6 fusion.93
  197.5 4.1 %fusion.18 = bf16[1088,768]{1,0:T(8,128)(2,1)} fusion(bf16[1088,768]{1,0:T(8,128)(2,1)} %all-gather.11.cloned.1.call-done, s32[]{:T(128)S(6)} %select_n.60, bf16[136,3072]{1,0:T(8,128)(2,1)} %copy-done.8, bf16[3072,768]{1,0:T(8,128)(2,1)} %param.29), kind=kOutput, calls=%fused_computation.28 | convolution fusion | flops 641832960 | bytes 5763076 | tf_op jit(solution)/shard_map/dot_general | solution.py:179
  201.6 3.8 %copy.94 = bf16[1088,768]{0,1:T(8,128)(2,1)} copy(bf16[1088,768]{1,0:T(8,128)(2,1)} %fusion.18) | data formatting | bytes 3342336 | tf_op jit(solution)/shard_map/dynamic_update_slice | solution.py:57
  205.5 3.7 %fusion.34 = bf16[6,17,8,128]{3,2,1,0:T(8,128)(2,1)S(1)} fusion(bf16[1088,6,128]{0,2,1:T(8,128)(2,1)} %bitcast.154, f32[6,136,1088]{2,1,0:T(8,128)} %copy-done.6, f32[6,136]{1,0:T(8,128)} %copy-done.24, f32[136,6]{0,1:T(8,128)} %bitcast.194), kind=kOutput, calls=%fused_computation.35 | convolution fusion | flops 229263360 | bytes 5437824 | tf_op jit(solution)/shard_map/hqk,khd->qhd/dot_general | solution.py:68
  209.2 4.1 %convolution_convert_fusion = bf16[136,3072]{1,0:T(8,128)(2,1)} fusion(bf16[768,3072]{1,0:T(8,128)(2,1)} %param.34, bf16[6,17,8,128]{3,2,1,0:T(8,128)(2,1)S(1)} %fusion.34), kind=kOutput, calls=%fused_computation.5 | convolution fusion | flops 642146304 | bytes 5763072 | tf_op jit(solution)/shard_map/dot_general | solution.py:83
  213.3 15.0 %fusion.1 = bf16[40,3072]{1,0:T(8,128)(2,1)} fusion(bf16[136,3072]{1,0:T(8,128)(2,1)} %convolution_convert_fusion), kind=kCustom, calls=%all-reduce-scatter.1 | all-reduce-scatter fusion | flops 491521 | bytes 1081856
  229.3 1.9 collective-permute-start.5
  231.8 4.0 %collective-permute-done.5 = bf16[18,3072]{1,0:T(8,128)(2,1)} collective-permute-done((bf16[18,3072]{1,0:T(8,128)(2,1)S(1)}, bf16[18,3072]{1,0:T(8,128)(2,1)}, u32[]{:S(2)}, u32[]{:S(2)}) %collective-permute-start.5) | collective-permute-done | bytes 110624
  235.8 5.4 %concatenate.140 = bf16[58,3072]{1,0:T(8,128)(2,1)} concatenate(bf16[18,3072]{1,0:T(8,128)(2,1)} %collective-permute-done.5, bf16[40,3072]{1,0:T(8,128)(2,1)} %fusion.1), dimensions={0} | concatenate | bytes 712704
  244.6 5.3 %all-gather.1 = f32[4,34,128]{2,1,0:T(8,128)S(1)} all-gather(f32[1,34,128]{2,1,0:T(8,128)S(1)} %convolution_bitcast_fusion), channel_id=1, replica_groups=mesh['patch'=8,'tile'=4] {'tile'}, dimensions={0}, use_global_device_ids=true | all-gather | bytes 87040 | tf_op jit(solution)/shard_map/all_gather | solution.py:90
  254.2 29.8 %all_gather.27 = bf16[1024,128]{1,0:T(8,128)(2,1)} all-gather(bf16[128,128]{1,0:T(8,128)(2,1)S(1)} %slice.284), channel_id=1, replica_groups=mesh['patch'=8,'tile'=4] {'patch'}, dimensions={0}, use_global_device_ids=true | all-gather | bytes 294912 | tf_op jit(solution)/shard_map/all_gather | solution.py:113
  285.6 4.6 %collective-permute-start.1 = (bf16[8,1,2,128]{3,2,1,0:T(2,128)(2,1)S(1)}, bf16[8,1,2,128]{3,2,1,0:T(2,128)(2,1)S(1)}, u32[]{:S(2)}, u32[]{:S(2)}) collective-permute-start(bf16[8,1,2,128]{3,2,1,0:T(2,128)(2,1)S(1)} %get-tuple-element.49), channel_id=1, source_target_pairs={{4,0},{8,4},{12,8},{16,12},{20,16},{24,20},{28,24},{5,1},{9,5},{13... | collective-permute-start | bytes 12296 | tf_op jit(solution)/shard_map/ppermute | solution.py:22
  290.3 1.9 collective-permute-start
  292.2 4.5 %collective-permute-done = bf16[8,1,2,128]{3,2,1,0:T(2,128)(2,1)S(1)} collective-permute-done((bf16[8,1,2,128]{3,2,1,0:T(2,128)(2,1)S(1)}, bf16[8,1,2,128]{3,2,1,0:T(2,128)(2,1)S(1)}, u32[]{:S(2)}, u32[]{:S(2)}) %collective-permute-start) | collective-permute-done | bytes 4128 | tf_op jit(solution)/shard_map/ppermute | solution.py:21
  298.7 2.4 collective-permute-start.2
  301.1 2.6 collective-permute-done.2
  (184 shorter events, 82.0 us)
Async XLA Ops:
  7.2 297.2 %copy-start = (bf16[3,3,3,128,512]{4,3,2,1,0:T(8,128)(2,1)S(1)}, bf16[3,3,3,128,512]{4,3,2,1,0:T(8,128)(2,1)}, u32[]{:S(2)}) copy-start(bf16[3,3,3,128,512]{4,3,2,1,0:T(8,128)(2,1)} %param.38) | copy-start | bytes 10616836
  7.2 49.6 %all-gather.7.cloned.1.call-start = ((), (), s32[]{:S(2)}) async-start(), calls=%async_computation | async-start | bytes 1880064 | tf_op jit(solution)/shard_map/all_gather | solution.py:54
  7.9 95.0 %all-gather.9.cloned.1.call-start = ((), (), s32[]{:S(2)}) async-start(), calls=%async_computation.1 | async-start | bytes 1880064 | tf_op jit(solution)/shard_map/all_gather | solution.py:53
  8.7 177.5 %all-gather.13.cloned.1.call-start = ((), (), s32[]{:S(2)}) async-start(), calls=%async_computation.3 | async-start | bytes 1880064 | tf_op jit(solution)/shard_map/all_gather | solution.py:53
  8.7 3.9 %copy-start.25 = (f32[2,3072]{1,0:T(2,128)S(1)}, f32[2,3072]{1,0:T(2,128)}, u32[]{:S(2)}) copy-start(f32[2,3072]{1,0:T(2,128)} %param.26) | copy-start | bytes 73732
  8.7 4.5 %copy-start.26 = (f32[2,3072]{1,0:T(2,128)S(1)}, f32[2,3072]{1,0:T(2,128)}, u32[]{:S(2)}) copy-start(f32[2,3072]{1,0:T(2,128)} %param.25) | copy-start | bytes 73732
  11.0 3.1 copy-start.9
  11.0 4.3 %copy-start.5 = (bf16[3072,768]{1,0:T(8,128)(2,1)S(1)}, bf16[3072,768]{1,0:T(8,128)(2,1)}, u32[]{:S(2)}) copy-start(bf16[3072,768]{1,0:T(8,128)(2,1)} %param.28) | copy-start | bytes 14155780
  31.8 2.7 copy-start.16
  31.8 2.7 copy-start.18
  33.3 2.8 copy-start.28
  33.3 3.6 %copy-start.31 = (u32[32]{0:T(128)S(1)}, u32[32]{0:T(128)}, u32[]{:S(2)}) copy-start(u32[32]{0:T(128)} %constant.105) | copy-start | bytes 388
  36.1 161.4 %all-gather.11.cloned.1.call-start = ((), (), s32[]{:S(2)}) async-start(), calls=%async_computation.2 | async-start | bytes 1880064 | tf_op jit(solution)/shard_map/all_gather | solution.py:54
  108.6 5.4 %slice-start = ((s8[4718592]{0:T(1024)(128)(4,1)}), s8[4194304]{0:T(1024)(128)(4,1)S(1)}, s32[]{:S(2)}) async-start(s8[4718592]{0:T(1024)(128)(4,1)} %bitcast.149), calls=%async_computation.4 | async-start | bytes 8388608
  111.3 2.7 slice-start.1
  114.0 19.5 %copy-start.30 = (f32[2]{0:T(128)S(1)}, f32[2]{0:T(128)}, u32[]{:S(2)}) copy-start(f32[2]{0:T(128)} %param.37) | copy-start | bytes 28
  130.0 15.5 %copy-start.21 = (f32[3072]{0:T(1024)S(1)}, f32[3072]{0:T(1024)}, u32[]{:S(2)}) copy-start(f32[3072]{0:T(1024)} %param.35) | copy-start | bytes 36868
  131.6 6.8 %collective-permute-start.4 = (bf16[18,3072]{1,0:T(8,128)(2,1)}, bf16[18,3072]{1,0:T(8,128)(2,1)}, u32[]{:S(2)}, u32[]{:S(2)}) collective-permute-start(bf16[18,3072]{1,0:T(8,128)(2,1)} %slice.255), channel_id=1, source_target_pairs={{0,1},{1,2},{2,3},{4,5},{5,6},{6,7},{8,9},{9,10},{10,11},{12,13},{... | collective-permute-start | bytes 331784
  158.4 1.8 copy-start.11
  158.4 1.8 copy-start.22
  158.4 1.8 copy-start.23
  171.4 11.1 %copy-start.27 = (f32[768]{0:T(1024)S(1)}, f32[768]{0:T(1024)}, u32[]{:S(2)}) copy-start(f32[768]{0:T(1024)} %param.30) | copy-start | bytes 9220
  181.0 3.8 %copy-start.17 = (f32[136,64]{1,0:T(8,128)S(1)}, f32[136,64]{1,0:T(8,128)}, u32[]{:S(2)}) copy-start(f32[136,64]{1,0:T(8,128)} %copy-done.16) | copy-start | bytes 104452
  181.0 3.8 %copy-start.19 = (f32[136,64]{1,0:T(8,128)S(1)}, f32[136,64]{1,0:T(8,128)}, u32[]{:S(2)}) copy-start(f32[136,64]{1,0:T(8,128)} %copy-done.18) | copy-start | bytes 104452
  194.3 1.8 copy-start.6
  194.3 1.8 copy-start.24
  229.3 6.6 %collective-permute-start.5 = (bf16[18,3072]{1,0:T(8,128)(2,1)S(1)}, bf16[18,3072]{1,0:T(8,128)(2,1)}, u32[]{:S(2)}, u32[]{:S(2)}) collective-permute-start(bf16[18,3072]{1,0:T(8,128)(2,1)S(1)} %slice.256), channel_id=1, source_target_pairs={{0,1},{1,2},{2,3},{4,5},{5,6},{6,7},{8,9},{9,10},{10,11},{12,13},{... | collective-permute-start | bytes 331784
  244.6 59.8 %copy-start.29 = (f32[512]{0:T(512)S(1)}, f32[512]{0:T(512)}, u32[]{:S(2)}) copy-start(f32[512]{0:T(512)} %param.39) | copy-start | bytes 6148
  285.6 6.5 %collective-permute-start.1 = (bf16[8,1,2,128]{3,2,1,0:T(2,128)(2,1)S(1)}, bf16[8,1,2,128]{3,2,1,0:T(2,128)(2,1)S(1)}, u32[]{:S(2)}, u32[]{:S(2)}) collective-permute-start(bf16[8,1,2,128]{3,2,1,0:T(2,128)(2,1)S(1)} %get-tuple-element.49), channel_id=1, source_target_pairs={{4,0},{8,4},{12,8},{16,12},{20,16},{24,20},{28,24},{5,1},{9,5},{13... | collective-permute-start | bytes 12296 | tf_op jit(solution)/shard_map/ppermute | solution.py:22
  290.3 6.4 %collective-permute-start = (bf16[8,1,2,128]{3,2,1,0:T(2,128)(2,1)S(1)}, bf16[8,1,2,128]{3,2,1,0:T(2,128)(2,1)S(1)}, u32[]{:S(2)}, u32[]{:S(2)}) collective-permute-start(bf16[8,1,2,128]{3,2,1,0:T(2,128)(2,1)S(1)} %get-tuple-element.48), channel_id=1, source_target_pairs={{0,4},{4,8},{8,12},{12,16},{16,20},{20,24},{24,28},{1,5},{5,9},{9,... | collective-permute-start | bytes 12296 | tf_op jit(solution)/shard_map/ppermute | solution.py:21
  296.7 4.3 %collective-permute-start.3 = (bf16[8,4,1,128]{3,2,1,0:T(2,128)(2,1)S(1)}, bf16[8,4,1,128]{3,2,1,0:T(2,128)(2,1)S(1)}, u32[]{:S(2)}, u32[]{:S(2)}) collective-permute-start(bf16[8,4,1,128]{3,2,1,0:T(2,128)(2,1)S(1)} %get-tuple-element.45), channel_id=1, source_target_pairs={{1,0},{2,1},{3,2},{5,4},{6,5},{7,6},{9,8},{10,9},{11,10},{13,12},{... | collective-permute-start | bytes 24584 | tf_op jit(solution)/shard_map/ppermute | solution.py:22
  298.7 5.1 %collective-permute-start.2 = (bf16[8,4,1,128]{3,2,1,0:T(2,128)(2,1)S(1)}, bf16[8,4,1,128]{3,2,1,0:T(2,128)(2,1)S(1)}, u32[]{:S(2)}, u32[]{:S(2)}) collective-permute-start(bf16[8,4,1,128]{3,2,1,0:T(2,128)(2,1)S(1)} %get-tuple-element.44), channel_id=1, source_target_pairs={{0,1},{1,2},{2,3},{4,5},{5,6},{6,7},{8,9},{9,10},{10,11},{12,13},{... | collective-permute-start | bytes 24584 | tf_op jit(solution)/shard_map/ppermute | solution.py:21
  (12 other events, 15.3 us)
Sparse Core Ops, SparseCore 0:
  10.2 46.5 all-gather.6
  59.0 43.8 all-gather.8
  105.1 43.8 all-gather.12
  151.1 43.8 all-gather.10
where the time goes:
time: 316 us; the launch traced here: 314 us
  waiting for transfers between devices  73.5 us (23%)
  blocking collectives  69.9 us (22%)
  local copies, waits for them, and re-layouts  56.3 us (18%)
  matrix products  48.8 us (15%)
  other arithmetic  35.3 us (11%)
  between operations  15 us (5%)
  starting transfers between devices  14.8 us (5%)
    all_gather x2, waiting for transfers between devices, attend_whole(): lax.all_gather(stale_keys, 'patch', axis=0, tiled=True)  38.1 us
    all_gather x1, blocking collectives, decode(): every_video = lax.all_gather(video_rows, 'patch', axis=0, tiled=True)  29.8 us
    unnamed x2, blocking collectives  29.3 us
    unnamed x99, local copies, waits for them, and re-layouts  21 us
    all_gather x2, waiting for transfers between devices, attend_whole(): lax.all_gather(stale_values, 'patch', axis=0, tiled=True)  18.7 us
    dot_general x4, matrix products, head_project(): raw_out = jnp.dot(normed, weight, preferred_element_type=jnp.float32)  14 us
    reduce_sum x8, other arithmetic, row_scaled(): jnp.mean(matrix * matrix, axis=-1, keepdims=True) + EPSILON  11.3 us
    all_gather x2, blocking collectives, velocity_of(): return lax.all_gather(own_velocity, 'tile', axis=0, tiled=True)  10.8 us
  transfers between devices with their start and end apart: 10, of which 6 were waited for; matrix products, arithmetic and copies ran while one was open for 36% of the time, Pallas kernels for 0%

commit v1 on v0

--- a/solution.py
+++ b/solution.py
@@ -9,6 +9,27 @@
 FRAMES = 8
 BH = 2
 EPSILON = 1e-06
+
+
+def collect(array, axis, dim):
+    size, index, extent = (lax.axis_size(axis), lax.axis_index(axis), array.shape[dim])
+    ahead = [(i, (i + 1) % size) for i in range(size)]
+    downward = [(i, (i - 1) % size) for i in range(size)]
+    out = jnp.zeros((*array.shape[:dim], size * extent, *array.shape[dim + 1 :]), array.dtype)
+    out = lax.dynamic_update_slice_in_dim(out, array, index * extent, axis=dim)
+    from_left = from_right = array
+    halfway = size // 2
+    for lap in range(1, halfway + 1):
+        from_left = lax.ppermute(from_left, axis, ahead)
+        out = lax.dynamic_update_slice_in_dim(
+            out, from_left, (index - lap) % size * extent, axis=dim
+        )
+        if lap < size - halfway:
+            from_right = lax.ppermute(from_right, axis, downward)
+            out = lax.dynamic_update_slice_in_dim(
+                out, from_right, (index + lap) % size * extent, axis=dim
+            )
+    return out
 
 
 def with_halo(shard, sides, width):
@@ -51,7 +72,7 @@
 def attend_whole(queries, fresh_keys, values, stale_keys, stale_values, row_start):
     every_keys, every_values = (
         lax.all_gather(stale_keys, "patch", axis=0, tiled=True),
-        lax.all_gather(stale_values, "patch", axis=0, tiled=True),
+        collect(stale_values, "patch", 0),
     )
     every_keys = lax.dynamic_update_slice_in_dim(every_keys, fresh_keys, row_start, 0)
     every_values = lax.dynamic_update_slice_in_dim(every_values, values, row_start, 0)

time: 316 us -> 407 us (1.29)
  local copies, waits for them, and re-layouts: 56.3 us -> 171 us
  waiting for transfers between devices: 73.5 us -> 29.9 us
  starting transfers between devices: 14.8 us -> 35.9 us
  matrix products: 48.8 us -> 41.3 us
    dynamic_update_slice x0 -> x16, local copies, waits for them, and re-layouts: none -> 80.1 us  [the longest x8 39 us: collect(): lax.dynamic_update_slice_in_dim(out, from_left, (index - lap) % size * ex...]
    all_gather x2, waiting for transfers between devices: 38.1 us -> 0.01 us  [attend_whole(): lax.all_gather(stale_keys, 'patch', axis=0, tiled=True)]
    ppermute x0 -> x14, local copies, waits for them, and re-layouts: none -> 26.1 us  [the longest x8 14.9 us: collect(): from_left = lax.ppermute(from_left, axis, ahead)]
    ppermute x0 -> x14, starting transfers between devices: none -> 19.1 us  [the longest x8 12.4 us: collect(): from_left = lax.ppermute(from_left, axis, ahead)]
    ppermute x0 -> x14, waiting for transfers between devices: none -> 18.8 us  [the longest x6 12.9 us: collect(): from_right = lax.ppermute(from_right, axis, downward)]
    all_gather x2 -> x0, waiting for transfers between devices: 18.7 us -> none  [attend_whole(): lax.all_gather(stale_values, 'patch', axis=0, tiled=True)]
    unnamed x6 -> x4, waiting for transfers between devices: 9.63 us -> 4.01 us
    unnamed x99 -> x104, local copies, waits for them, and re-layouts: 21 us -> 20.8 us
  transfers between devices with their start and end apart: 10 -> 22, of which waited for: 6 -> 6; matrix products, arithmetic and copies ran while one was open for 36% -> 55% of each run, Pallas kernels for 0% -> 0%
where the time goes in v1:
time: 407 us; the launch traced here: 402 us
  local copies, waits for them, and re-layouts  171 us (42%)
  blocking collectives  73.3 us (18%)
  matrix products  41.3 us (10%)
  starting transfers between devices  35.9 us (9%)
  other arithmetic  34.7 us (9%)
  waiting for transfers between devices  29.9 us (7%)
  between operations  15.4 us (4%)
    dynamic_update_slice x8, local copies, waits for them, and re-layouts, collect(): lax.dynamic_update_slice_in_dim(out, from_left, (index - lap) % size * ex...  39 us
    all_gather x1, blocking collectives, decode(): every_video = lax.all_gather(video_rows, 'patch', axis=0, tiled=True)  33.2 us
    dynamic_update_slice x6, local copies, waits for them, and re-layouts, collect(): lax.dynamic_update_slice_in_dim(out, from_right, (index + lap) % size * e...  30.8 us
    unnamed x2, blocking collectives  29.2 us
    unnamed x104, local copies, waits for them, and re-layouts  20.8 us
    ppermute x8, local copies, waits for them, and re-layouts, collect(): from_left = lax.ppermute(from_left, axis, ahead)  14.9 us
    dot_general x4, matrix products, head_project(): raw_out = jnp.dot(normed, weight, preferred_element_type=jnp.float32)  14.3 us
    ppermute x6, waiting for transfers between devices, collect(): from_right = lax.ppermute(from_right, axis, downward)  12.9 us
  transfers between devices with their start and end apart: 22, of which 6 were waited for; matrix products, arithmetic and copies ran while one was open for 55% of the time, Pallas kernels for 0%

profile of v1, /device:TPU:12, one launch (start us, length us, event | category | flops | bytes accessed | tf_op | source)
XLA Modules:
  0.0 401.9 jit_solution(17884331751384168004)
XLA Ops:
  26.9 4.2 %fusion.93 = f32[136,768]{1,0:T(8,128)} fusion(bf16[136,3072]{1,0:T(8,128)(2,1)} %copy-done.7, bf16[3072,768]{1,0:T(8,128)(2,1)} %param.27), kind=kOutput, calls=%fused_computation.192 | convolution fusion | flops 641728512 | bytes 5971968 | tf_op jit(solution)/shard_map/dot_general | solution.py:66
  47.7 5.1 %dynamic_update_slice.60 = bf16[1088,768]{0,1:T(8,128)(2,1)} dynamic-update-slice(bf16[1088,768]{0,1:T(8,128)(2,1)} %broadcast.302.clone, bf16[136,768]{0,1:T(8,128)(2,1)} %copy.130, s32[]{:T(128)S(6)} %select_n.134, s32[]{:T(128)} %constant.135.clone.1) | dynamic-update-slice | bytes 417796 | tf_op jit(solution)/shard_map/dynamic_update_slice | solution.py:19
  54.2 5.2 %dynamic_update_slice.70 = bf16[1088,768]{0,1:T(8,128)(2,1)} dynamic-update-slice(bf16[1088,768]{0,1:T(8,128)(2,1)} %broadcast.302.clone.1, bf16[136,768]{0,1:T(8,128)(2,1)} %copy.138, s32[]{:T(128)S(6)} %select_n.134, s32[]{:T(128)} %constant.135.clone.1) | dynamic-update-slice | bytes 417796 | tf_op jit(solution)/shard_map/dynamic_update_slice | solution.py:19
  65.5 12.9 %collective-permute-done.3 = bf16[136,768]{1,0:T(8,128)(2,1)} collective-permute-done((bf16[136,768]{1,0:T(8,128)(2,1)}, bf16[136,768]{1,0:T(8,128)(2,1)}, u32[]{:S(2)}, u32[]{:S(2)}) %collective-permute-start.3) | collective-permute-done | bytes 208928 | tf_op jit(solution)/shard_map/ppermute | solution.py:28
  82.6 4.2 %collective-permute-done.4 = bf16[136,768]{1,0:T(8,128)(2,1)} collective-permute-done((bf16[136,768]{1,0:T(8,128)(2,1)}, bf16[136,768]{1,0:T(8,128)(2,1)}, u32[]{:S(2)}, u32[]{:S(2)}) %collective-permute-start.4) | collective-permute-done | bytes 208928 | tf_op jit(solution)/shard_map/ppermute | solution.py:23
  91.7 5.1 %dynamic_update_slice.61 = bf16[1088,768]{0,1:T(8,128)(2,1)} dynamic-update-slice(bf16[1088,768]{0,1:T(8,128)(2,1)} %dynamic_update_slice.60, bf16[136,768]{0,1:T(8,128)(2,1)} %copy.131, s32[]{:T(128)S(6)} %select_n.136, s32[]{:T(128)} %constant.135.clone.1) | dynamic-update-slice | bytes 417796 | tf_op jit(solution)/shard_map/dynamic_update_slice | solution.py:24
  98.7 5.1 %dynamic_update_slice.62 = bf16[1088,768]{0,1:T(8,128)(2,1)} dynamic-update-slice(bf16[1088,768]{0,1:T(8,128)(2,1)} %dynamic_update_slice.61, bf16[136,768]{0,1:T(8,128)(2,1)} %copy.132, s32[]{:T(128)S(6)} %select_n.138, s32[]{:T(128)} %constant.135.clone.1) | dynamic-update-slice | bytes 417796 | tf_op jit(solution)/shard_map/dynamic_update_slice | solution.py:29
  105.7 4.7 %dynamic_update_slice.63 = bf16[1088,768]{0,1:T(8,128)(2,1)} dynamic-update-slice(bf16[1088,768]{0,1:T(8,128)(2,1)} %dynamic_update_slice.62, bf16[136,768]{0,1:T(8,128)(2,1)} %copy.133, s32[]{:T(128)S(6)} %select_n.140, s32[]{:T(128)} %constant.135.clone.1) | dynamic-update-slice | bytes 417796 | tf_op jit(solution)/shard_map/dynamic_update_slice | solution.py:24
  112.2 5.1 %dynamic_update_slice.64 = bf16[1088,768]{0,1:T(8,128)(2,1)} dynamic-update-slice(bf16[1088,768]{0,1:T(8,128)(2,1)} %dynamic_update_slice.63, bf16[136,768]{0,1:T(8,128)(2,1)} %copy.134, s32[]{:T(128)S(6)} %select_n.142, s32[]{:T(128)} %constant.135.clone.1) | dynamic-update-slice | bytes 417796 | tf_op jit(solution)/shard_map/dynamic_update_slice | solution.py:29
  119.3 4.6 %dynamic_update_slice.65 = bf16[1088,768]{0,1:T(8,128)(2,1)} dynamic-update-slice(bf16[1088,768]{0,1:T(8,128)(2,1)} %dynamic_update_slice.64, bf16[136,768]{0,1:T(8,128)(2,1)} %copy.135, s32[]{:T(128)S(6)} %select_n.144, s32[]{:T(128)} %constant.135.clone.1) | dynamic-update-slice | bytes 417796 | tf_op jit(solution)/shard_map/dynamic_update_slice | solution.py:24
  125.7 5.1 %dynamic_update_slice.66 = bf16[1088,768]{0,1:T(8,128)(2,1)} dynamic-update-slice(bf16[1088,768]{0,1:T(8,128)(2,1)} %dynamic_update_slice.65, bf16[136,768]{0,1:T(8,128)(2,1)} %copy.136, s32[]{:T(128)S(6)} %select_n.146, s32[]{:T(128)} %constant.135.clone.1) | dynamic-update-slice | bytes 417796 | tf_op jit(solution)/shard_map/dynamic_update_slice | solution.py:29
  134.8 5.1 %dynamic_update_slice.67 = bf16[1088,768]{0,1:T(8,128)(2,1)} dynamic-update-slice(bf16[1088,768]{0,1:T(8,128)(2,1)} %dynamic_update_slice.66, bf16[136,768]{0,1:T(8,128)(2,1)} %copy.137, s32[]{:T(128)S(6)} %select_n.148, s32[]{:T(128)} %constant.135.clone.1) | dynamic-update-slice | bytes 417796 | tf_op jit(solution)/shard_map/dynamic_update_slice | solution.py:24
  139.9 5.1 %dynamic_update_slice.68 = bf16[1088,768]{0,1:T(8,128)(2,1)} dynamic-update-slice(bf16[1088,768]{0,1:T(8,128)(2,1)} %dynamic_update_slice.67, bf16[136,768]{0,1:T(8,128)(2,1)} %copy.138, s32[]{:T(128)S(6)} %select_n.134, s32[]{:T(128)} %constant.135.clone.1) | dynamic-update-slice | bytes 417796 | tf_op jit(solution)/shard_map/dynamic_update_slice | solution.py:78
  157.8 13.9 %fusion = bf16[40,3072]{1,0:T(8,128)(2,1)} fusion(bf16[136,3072]{1,0:T(8,128)(2,1)} %convolution_convert_fusion.1), kind=kCustom, calls=%all-reduce-scatter | all-reduce-scatter fusion | flops 491521 | bytes 1081856
  177.7 5.2 %dynamic_update_slice.71 = bf16[1088,768]{0,1:T(8,128)(2,1)} dynamic-update-slice(bf16[1088,768]{0,1:T(8,128)(2,1)} %dynamic_update_slice.70, bf16[136,768]{0,1:T(8,128)(2,1)} %copy.149, s32[]{:T(128)S(6)} %select_n.136, s32[]{:T(128)} %constant.135.clone.1) | dynamic-update-slice | bytes 417796 | tf_op jit(solution)/shard_map/dynamic_update_slice | solution.py:24
  184.8 5.1 %dynamic_update_slice.72 = bf16[1088,768]{0,1:T(8,128)(2,1)} dynamic-update-slice(bf16[1088,768]{0,1:T(8,128)(2,1)} %dynamic_update_slice.71, bf16[136,768]{0,1:T(8,128)(2,1)} %copy.150, s32[]{:T(128)S(6)} %select_n.138, s32[]{:T(128)} %constant.135.clone.1) | dynamic-update-slice | bytes 417796 | tf_op jit(solution)/shard_map/dynamic_update_slice | solution.py:29
  191.8 4.7 %dynamic_update_slice.73 = bf16[1088,768]{0,1:T(8,128)(2,1)} dynamic-update-slice(bf16[1088,768]{0,1:T(8,128)(2,1)} %dynamic_update_slice.72, bf16[136,768]{0,1:T(8,128)(2,1)} %copy.151, s32[]{:T(128)S(6)} %select_n.140, s32[]{:T(128)} %constant.135.clone.1) | dynamic-update-slice | bytes 417796 | tf_op jit(solution)/shard_map/dynamic_update_slice | solution.py:24
  198.3 5.2 %dynamic_update_slice.74 = bf16[1088,768]{0,1:T(8,128)(2,1)} dynamic-update-slice(bf16[1088,768]{0,1:T(8,128)(2,1)} %dynamic_update_slice.73, bf16[136,768]{0,1:T(8,128)(2,1)} %copy.152, s32[]{:T(128)S(6)} %select_n.142, s32[]{:T(128)} %constant.135.clone.1) | dynamic-update-slice | bytes 417796 | tf_op jit(solution)/shard_map/dynamic_update_slice | solution.py:29
  205.3 4.6 %dynamic_update_slice.75 = bf16[1088,768]{0,1:T(8,128)(2,1)} dynamic-update-slice(bf16[1088,768]{0,1:T(8,128)(2,1)} %dynamic_update_slice.74, bf16[136,768]{0,1:T(8,128)(2,1)} %copy.153, s32[]{:T(128)S(6)} %select_n.144, s32[]{:T(128)} %constant.135.clone.1) | dynamic-update-slice | bytes 417796 | tf_op jit(solution)/shard_map/dynamic_update_slice | solution.py:24
  211.8 5.2 %dynamic_update_slice.76 = bf16[1088,768]{0,1:T(8,128)(2,1)} dynamic-update-slice(bf16[1088,768]{0,1:T(8,128)(2,1)} %dynamic_update_slice.75, bf16[136,768]{0,1:T(8,128)(2,1)} %copy.154, s32[]{:T(128)S(6)} %select_n.146, s32[]{:T(128)} %constant.135.clone.1) | dynamic-update-slice | bytes 417796 | tf_op jit(solution)/shard_map/dynamic_update_slice | solution.py:29
  218.8 5.1 %dynamic_update_slice.77 = bf16[1088,768]{0,1:T(8,128)(2,1)} dynamic-update-slice(bf16[1088,768]{0,1:T(8,128)(2,1)} %dynamic_update_slice.76, bf16[136,768]{0,1:T(8,128)(2,1)} %copy.155, s32[]{:T(128)S(6)} %select_n.148, s32[]{:T(128)} %constant.135.clone.1) | dynamic-update-slice | bytes 417796 | tf_op jit(solution)/shard_map/dynamic_update_slice | solution.py:24
  223.9 5.4 %concatenate.139 = bf16[58,3072]{1,0:T(8,128)(2,1)} concatenate(bf16[18,3072]{1,0:T(8,128)(2,1)} %collective-permute-done.18, bf16[40,3072]{1,0:T(8,128)(2,1)} %fusion), dimensions={0} | concatenate | bytes 712704
  232.7 5.6 %all-gather = f32[4,34,128]{2,1,0:T(8,128)S(1)} all-gather(f32[1,34,128]{2,1,0:T(8,128)S(1)} %convolution_bitcast_fusion.1), channel_id=1, replica_groups=mesh['patch'=8,'tile'=4] {'tile'}, dimensions={0}, use_global_device_ids=true | all-gather | bytes 87040 | tf_op jit(solution)/shard_map/all_gather | solution.py:111
  253.3 4.2 %fusion.95 = f32[136,768]{1,0:T(8,128)} fusion(bf16[136,3072]{1,0:T(8,128)(2,1)} %copy-done.8, bf16[3072,768]{1,0:T(8,128)(2,1)} %param.27), kind=kOutput, calls=%fused_computation.194 | convolution fusion | flops 641728512 | bytes 5971968 | tf_op jit(solution)/shard_map/dot_general | solution.py:66
  262.9 4.2 %fusion.96 = f32[136,768]{1,0:T(8,128)} fusion(bf16[136,3072]{1,0:T(8,128)(2,1)} %copy-done.8, bf16[3072,768]{1,0:T(8,128)(2,1)} %param.28), kind=kOutput, calls=%fused_computation.195 | convolution fusion | flops 641728512 | bytes 5971968 | tf_op jit(solution)/shard_map/dot_general | solution.py:66
  283.3 5.1 %dynamic_update_slice.78 = bf16[1088,768]{0,1:T(8,128)(2,1)} dynamic-update-slice(bf16[1088,768]{0,1:T(8,128)(2,1)} %dynamic_update_slice.77, bf16[136,768]{0,1:T(8,128)(2,1)} %copy.156, s32[]{:T(128)S(6)} %select_n.134, s32[]{:T(128)} %constant.135.clone.1) | dynamic-update-slice | bytes 417796 | tf_op jit(solution)/shard_map/dynamic_update_slice | solution.py:78
  295.6 15.3 %fusion.1 = bf16[40,3072]{1,0:T(8,128)(2,1)} fusion(bf16[136,3072]{1,0:T(8,128)(2,1)} %convolution_convert_fusion), kind=kCustom, calls=%all-reduce-scatter.1 | all-reduce-scatter fusion | flops 491521 | bytes 1081856
  318.4 5.4 %concatenate.140 = bf16[58,3072]{1,0:T(8,128)(2,1)} concatenate(bf16[18,3072]{1,0:T(8,128)(2,1)} %collective-permute-done.19, bf16[40,3072]{1,0:T(8,128)(2,1)} %fusion.1), dimensions={0} | concatenate | bytes 712704
  327.2 5.3 %all-gather.1 = f32[4,34,128]{2,1,0:T(8,128)S(1)} all-gather(f32[1,34,128]{2,1,0:T(8,128)S(1)} %convolution_bitcast_fusion), channel_id=1, replica_groups=mesh['patch'=8,'tile'=4] {'tile'}, dimensions={0}, use_global_device_ids=true | all-gather | bytes 87040 | tf_op jit(solution)/shard_map/all_gather | solution.py:111
  336.8 33.2 %all_gather.19 = bf16[1024,128]{1,0:T(8,128)(2,1)} all-gather(bf16[128,128]{1,0:T(8,128)(2,1)S(1)} %slice.284), channel_id=1, replica_groups=mesh['patch'=8,'tile'=4] {'patch'}, dimensions={0}, use_global_device_ids=true | all-gather | bytes 294912 | tf_op jit(solution)/shard_map/all_gather | solution.py:134
  371.6 6.6 %collective-permute-start.15 = (bf16[8,1,2,128]{3,2,1,0:T(2,128)(2,1)S(1)}, bf16[8,1,2,128]{3,2,1,0:T(2,128)(2,1)S(1)}, u32[]{:S(2)}, u32[]{:S(2)}) collective-permute-start(bf16[8,1,2,128]{3,2,1,0:T(2,128)(2,1)S(1)} %get-tuple-element.49), channel_id=1, source_target_pairs={{4,0},{8,4},{12,8},{16,12},{20,16},{24,20},{28,24},{5,1},{9,5},{13... | collective-permute-start | bytes 12296 | tf_op jit(solution)/shard_map/ppermute | solution.py:43
  380.1 4.5 %collective-permute-done.14 = bf16[8,1,2,128]{3,2,1,0:T(2,128)(2,1)S(1)} collective-permute-done((bf16[8,1,2,128]{3,2,1,0:T(2,128)(2,1)S(1)}, bf16[8,1,2,128]{3,2,1,0:T(2,128)(2,1)S(1)}, u32[]{:S(2)}, u32[]{:S(2)}) %collective-permute-start.14) | collective-permute-done | bytes 4128 | tf_op jit(solution)/shard_map/ppermute | solution.py:42
  (246 shorter events, 171.2 us)
Async XLA Ops:
  7.2 385.1 %copy-start = (bf16[3,3,3,128,512]{4,3,2,1,0:T(8,128)(2,1)S(1)}, bf16[3,3,3,128,512]{4,3,2,1,0:T(8,128)(2,1)}, u32[]{:S(2)}) copy-start(bf16[3,3,3,128,512]{4,3,2,1,0:T(8,128)(2,1)} %param.38) | copy-start | bytes 10616836
  7.2 137.8 %all-gather.5.cloned.1.call-start = ((), (), s32[]{:S(2)}) async-start(), calls=%async_computation | async-start | bytes 1880064 | tf_op jit(solution)/shard_map/all_gather | solution.py:74
  7.2 31.2 %collective-permute-start = (bf16[136,768]{1,0:T(8,128)(2,1)}, bf16[136,768]{1,0:T(8,128)(2,1)}, u32[]{:S(2)}, u32[]{:S(2)}) collective-permute-start(bf16[136,768]{1,0:T(8,128)(2,1)} %param.33), channel_id=1, source_target_pairs={{0,4},{4,8},{8,12},{12,16},{16,20},{20,24},{24,28},{28,0},{1,5},{5... | collective-permute-start | bytes 626696 | tf_op jit(solution)/shard_map/ppermute | solution.py:23
  8.8 50.6 %collective-permute-start.1 = (bf16[136,768]{1,0:T(8,128)(2,1)}, bf16[136,768]{1,0:T(8,128)(2,1)}, u32[]{:S(2)}, u32[]{:S(2)}) collective-permute-start(bf16[136,768]{1,0:T(8,128)(2,1)} %param.33), channel_id=1, source_target_pairs={{0,28},{4,0},{8,4},{12,8},{16,12},{20,16},{24,20},{28,24},{1,29},{... | collective-permute-start | bytes 626696 | tf_op jit(solution)/shard_map/ppermute | solution.py:28
  10.2 267.4 %all-gather.7.cloned.1.call-start = ((), (), s32[]{:S(2)}) async-start(), calls=%async_computation.1 | async-start | bytes 1880064 | tf_op jit(solution)/shard_map/all_gather | solution.py:74
  10.3 4.5 %copy-start.26 = (f32[2,3072]{1,0:T(2,128)S(1)}, f32[2,3072]{1,0:T(2,128)}, u32[]{:S(2)}) copy-start(f32[2,3072]{1,0:T(2,128)} %param.25) | copy-start | bytes 73732
  17.5 44.7 %collective-permute-start.7 = (bf16[136,768]{1,0:T(8,128)(2,1)}, bf16[136,768]{1,0:T(8,128)(2,1)}, u32[]{:S(2)}, u32[]{:S(2)}) collective-permute-start(bf16[136,768]{1,0:T(8,128)(2,1)} %convolution_convert_fusion.3), channel_id=1, source_target_pairs={{0,4},{4,8},{8,12},{12,16},{16,20},{20,24},{24,28},{28,0},{1,5},{5... | collective-permute-start | bytes 626696 | tf_op jit(solution)/shard_map/ppermute | solution.py:23
  18.1 47.3 %collective-permute-start.8 = (bf16[136,768]{1,0:T(8,128)(2,1)}, bf16[136,768]{1,0:T(8,128)(2,1)}, u32[]{:S(2)}, u32[]{:S(2)}) collective-permute-start(bf16[136,768]{1,0:T(8,128)(2,1)} %convolution_convert_fusion.3), channel_id=1, source_target_pairs={{0,28},{4,0},{8,4},{12,8},{16,12},{20,16},{24,20},{28,24},{1,29},{... | collective-permute-start | bytes 626696 | tf_op jit(solution)/shard_map/ppermute | solution.py:28
  38.4 23.9 %collective-permute-start.2 = (bf16[136,768]{1,0:T(8,128)(2,1)}, bf16[136,768]{1,0:T(8,128)(2,1)}, u32[]{:S(2)}, u32[]{:S(2)}) collective-permute-start(bf16[136,768]{1,0:T(8,128)(2,1)} %collective-permute-done), channel_id=1, source_target_pairs={{0,4},{4,8},{8,12},{12,16},{16,20},{20,24},{24,28},{28,0},{1,5},{5... | collective-permute-start | bytes 626696 | tf_op jit(solution)/shard_map/ppermute | solution.py:23
  39.8 5.4 %copy-start.31 = (u32[32]{0:T(128)S(1)}, u32[32]{0:T(128)}, u32[]{:S(2)}) copy-start(u32[32]{0:T(128)} %constant.164) | copy-start | bytes 388
  47.7 17.5 %copy-start.28 = (s32[1024]{0:T(1024)S(1)}, s32[1024]{0:T(1024)}, u32[]{:S(2)}) copy-start(s32[1024]{0:T(1024)} %param.22) | copy-start | bytes 12292
  59.4 19.0 %collective-permute-start.3 = (bf16[136,768]{1,0:T(8,128)(2,1)}, bf16[136,768]{1,0:T(8,128)(2,1)}, u32[]{:S(2)}, u32[]{:S(2)}) collective-permute-start(bf16[136,768]{1,0:T(8,128)(2,1)} %collective-permute-done.1), channel_id=1, source_target_pairs={{0,28},{4,0},{8,4},{12,8},{16,12},{20,16},{24,20},{28,24},{1,29},{... | collective-permute-start | bytes 626696 | tf_op jit(solution)/shard_map/ppermute | solution.py:28
  62.2 17.9 %collective-permute-start.9 = (bf16[136,768]{1,0:T(8,128)(2,1)}, bf16[136,768]{1,0:T(8,128)(2,1)}, u32[]{:S(2)}, u32[]{:S(2)}) collective-permute-start(bf16[136,768]{1,0:T(8,128)(2,1)} %collective-permute-done.7), channel_id=1, source_target_pairs={{0,4},{4,8},{8,12},{12,16},{16,20},{20,24},{24,28},{28,0},{1,5},{5... | collective-permute-start | bytes 626696 | tf_op jit(solution)/shard_map/ppermute | solution.py:23
  62.3 24.5 %collective-permute-start.4 = (bf16[136,768]{1,0:T(8,128)(2,1)}, bf16[136,768]{1,0:T(8,128)(2,1)}, u32[]{:S(2)}, u32[]{:S(2)}) collective-permute-start(bf16[136,768]{1,0:T(8,128)(2,1)} %collective-permute-done.2), channel_id=1, source_target_pairs={{0,4},{4,8},{8,12},{12,16},{16,20},{20,24},{24,28},{28,0},{1,5},{5... | collective-permute-start | bytes 626696 | tf_op jit(solution)/shard_map/ppermute | solution.py:23
  65.4 52.0 %collective-permute-start.10 = (bf16[136,768]{1,0:T(8,128)(2,1)}, bf16[136,768]{1,0:T(8,128)(2,1)}, u32[]{:S(2)}, u32[]{:S(2)}) collective-permute-start(bf16[136,768]{1,0:T(8,128)(2,1)} %collective-permute-done.8), channel_id=1, source_target_pairs={{0,28},{4,0},{8,4},{12,8},{16,12},{20,16},{24,20},{28,24},{1,29},{... | collective-permute-start | bytes 626696 | tf_op jit(solution)/shard_map/ppermute | solution.py:28
  78.4 45.4 %collective-permute-start.5 = (bf16[136,768]{1,0:T(8,128)(2,1)}, bf16[136,768]{1,0:T(8,128)(2,1)}, u32[]{:S(2)}, u32[]{:S(2)}) collective-permute-start(bf16[136,768]{1,0:T(8,128)(2,1)} %collective-permute-done.3), channel_id=1, source_target_pairs={{0,28},{4,0},{8,4},{12,8},{16,12},{20,16},{24,20},{28,24},{1,29},{... | collective-permute-start | bytes 626696 | tf_op jit(solution)/shard_map/ppermute | solution.py:28
  80.1 50.7 %collective-permute-start.11 = (bf16[136,768]{1,0:T(8,128)(2,1)}, bf16[136,768]{1,0:T(8,128)(2,1)}, u32[]{:S(2)}, u32[]{:S(2)}) collective-permute-start(bf16[136,768]{1,0:T(8,128)(2,1)} %collective-permute-done.9), channel_id=1, source_target_pairs={{0,4},{4,8},{8,12},{12,16},{16,20},{20,24},{24,28},{28,0},{1,5},{5... | collective-permute-start | bytes 626696 | tf_op jit(solution)/shard_map/ppermute | solution.py:23
  86.8 46.1 %collective-permute-start.6 = (bf16[136,768]{1,0:T(8,128)(2,1)}, bf16[136,768]{1,0:T(8,128)(2,1)}, u32[]{:S(2)}, u32[]{:S(2)}) collective-permute-start(bf16[136,768]{1,0:T(8,128)(2,1)} %collective-permute-done.4), channel_id=1, source_target_pairs={{0,4},{4,8},{8,12},{12,16},{16,20},{20,24},{24,28},{28,0},{1,5},{5... | collective-permute-start | bytes 626696 | tf_op jit(solution)/shard_map/ppermute | solution.py:23
  117.4 92.5 %collective-permute-start.12 = (bf16[136,768]{1,0:T(8,128)(2,1)}, bf16[136,768]{1,0:T(8,128)(2,1)}, u32[]{:S(2)}, u32[]{:S(2)}) collective-permute-start(bf16[136,768]{1,0:T(8,128)(2,1)} %collective-permute-done.10), channel_id=1, source_target_pairs={{0,28},{4,0},{8,4},{12,8},{16,12},{20,16},{24,20},{28,24},{1,29},{... | collective-permute-start | bytes 626696 | tf_op jit(solution)/shard_map/ppermute | solution.py:28
  130.8 86.1 %collective-permute-start.13 = (bf16[136,768]{1,0:T(8,128)(2,1)}, bf16[136,768]{1,0:T(8,128)(2,1)}, u32[]{:S(2)}, u32[]{:S(2)}) collective-permute-start(bf16[136,768]{1,0:T(8,128)(2,1)} %collective-permute-done.11), channel_id=1, source_target_pairs={{0,4},{4,8},{8,12},{12,16},{16,20},{20,24},{24,28},{28,0},{1,5},{5... | collective-permute-start | bytes 626696 | tf_op jit(solution)/shard_map/ppermute | solution.py:23
  150.7 5.3 %slice-start = ((s8[4718592]{0:T(1024)(128)(4,1)}), s8[4194304]{0:T(1024)(128)(4,1)S(1)}, s32[]{:S(2)}) async-start(s8[4718592]{0:T(1024)(128)(4,1)} %bitcast.149), calls=%async_computation.2 | async-start | bytes 8388608
  156.0 19.2 %copy-start.30 = (f32[2]{0:T(128)S(1)}, f32[2]{0:T(128)}, u32[]{:S(2)}) copy-start(f32[2]{0:T(128)} %param.37) | copy-start | bytes 28
  173.3 50.6 %collective-permute-start.18 = (bf16[18,3072]{1,0:T(8,128)(2,1)}, bf16[18,3072]{1,0:T(8,128)(2,1)}, u32[]{:S(2)}, u32[]{:S(2)}) collective-permute-start(bf16[18,3072]{1,0:T(8,128)(2,1)} %slice.255), channel_id=1, source_target_pairs={{0,1},{1,2},{2,3},{4,5},{5,6},{6,7},{8,9},{9,10},{10,11},{12,13},{... | collective-permute-start | bytes 331784
  218.8 12.2 %copy-start.22 = (f32[3072]{0:T(1024)S(1)}, f32[3072]{0:T(1024)}, u32[]{:S(2)}) copy-start(f32[3072]{0:T(1024)} %param.35) | copy-start | bytes 36868
  262.9 11.0 %copy-start.27 = (f32[768]{0:T(1024)S(1)}, f32[768]{0:T(1024)}, u32[]{:S(2)}) copy-start(f32[768]{0:T(1024)} %param.30) | copy-start | bytes 9220
  288.4 5.3 %slice-start.2 = ((s8[4718592]{0:T(1024)(128)(4,1)}), s8[4194304]{0:T(1024)(128)(4,1)S(1)}, s32[]{:S(2)}) async-start(s8[4718592]{0:T(1024)(128)(4,1)} %bitcast.151), calls=%async_computation.4 | async-start | bytes 8388608
  311.8 6.6 %collective-permute-start.19 = (bf16[18,3072]{1,0:T(8,128)(2,1)S(1)}, bf16[18,3072]{1,0:T(8,128)(2,1)}, u32[]{:S(2)}, u32[]{:S(2)}) collective-permute-start(bf16[18,3072]{1,0:T(8,128)(2,1)S(1)} %slice.256), channel_id=1, source_target_pairs={{0,1},{1,2},{2,3},{4,5},{5,6},{6,7},{8,9},{9,10},{10,11},{12,13},{... | collective-permute-start | bytes 331784
  327.2 65.1 %copy-start.29 = (f32[512]{0:T(512)S(1)}, f32[512]{0:T(512)}, u32[]{:S(2)}) copy-start(f32[512]{0:T(512)} %param.39) | copy-start | bytes 6148
  371.6 8.5 %collective-permute-start.15 = (bf16[8,1,2,128]{3,2,1,0:T(2,128)(2,1)S(1)}, bf16[8,1,2,128]{3,2,1,0:T(2,128)(2,1)S(1)}, u32[]{:S(2)}, u32[]{:S(2)}) collective-permute-start(bf16[8,1,2,128]{3,2,1,0:T(2,128)(2,1)S(1)} %get-tuple-element.49), channel_id=1, source_target_pairs={{4,0},{8,4},{12,8},{16,12},{20,16},{24,20},{28,24},{5,1},{9,5},{13... | collective-permute-start | bytes 12296 | tf_op jit(solution)/shard_map/ppermute | solution.py:43
  378.2 6.4 %collective-permute-start.14 = (bf16[8,1,2,128]{3,2,1,0:T(2,128)(2,1)S(1)}, bf16[8,1,2,128]{3,2,1,0:T(2,128)(2,1)S(1)}, u32[]{:S(2)}, u32[]{:S(2)}) collective-permute-start(bf16[8,1,2,128]{3,2,1,0:T(2,128)(2,1)S(1)} %get-tuple-element.48), channel_id=1, source_target_pairs={{0,4},{4,8},{8,12},{12,16},{16,20},{20,24},{24,28},{1,5},{5,9},{9,... | collective-permute-start | bytes 12296 | tf_op jit(solution)/shard_map/ppermute | solution.py:42
  384.7 4.3 %collective-permute-start.17 = (bf16[8,4,1,128]{3,2,1,0:T(2,128)(2,1)S(1)}, bf16[8,4,1,128]{3,2,1,0:T(2,128)(2,1)S(1)}, u32[]{:S(2)}, u32[]{:S(2)}) collective-permute-start(bf16[8,4,1,128]{3,2,1,0:T(2,128)(2,1)S(1)} %get-tuple-element.45), channel_id=1, source_target_pairs={{1,0},{2,1},{3,2},{5,4},{6,5},{7,6},{9,8},{10,9},{11,10},{13,12},{... | collective-permute-start | bytes 24584 | tf_op jit(solution)/shard_map/ppermute | solution.py:43
  386.6 5.1 %collective-permute-start.16 = (bf16[8,4,1,128]{3,2,1,0:T(2,128)(2,1)S(1)}, bf16[8,4,1,128]{3,2,1,0:T(2,128)(2,1)S(1)}, u32[]{:S(2)}, u32[]{:S(2)}) collective-permute-start(bf16[8,4,1,128]{3,2,1,0:T(2,128)(2,1)S(1)} %get-tuple-element.44), channel_id=1, source_target_pairs={{0,1},{1,2},{2,3},{4,5},{5,6},{6,7},{8,9},{9,10},{10,11},{12,13},{... | collective-permute-start | bytes 24584 | tf_op jit(solution)/shard_map/ppermute | solution.py:42
  (26 other events, 56.3 us)
Sparse Core Ops, SparseCore 0:
  10.3 54.1 all-gather.4
  66.7 49.1 all-gather.6
